TPU v7x, 512 devices: a whole 4x4x16 slice. The times are simulated.
512 devices in a mesh: shape: 16 (over z_lo, x), query: 32 (over z_hi, y, core).
Axes of the slice: x: 4, y: 4, z: 16 (z_hi: 4, z_lo: 4; z = z_hi * 4 + z_lo), core: 2. Of those that a mesh axis runs over, the one named last changes fastest.
Arguments:
- queries: bfloat16 [16, 4096, 512], P('shape', 'query'), may hold values from -128 to 128
- keys: bfloat16 [16, 1024, 512], P('shape', 'query'), may hold values from -5 to 5
- values: bfloat16 [16, 1024, 512], P('shape', 'query'), may hold values from -6 to 6
- out_weight: bfloat16 [512, 512], replicated, may hold values from -0.25 to 0.25
- out_grad: float32 [16, 4096, 512], P('shape', 'query'), may hold values from -6 to 6
Outputs:
- query_grad: float32 [16, 4096, 512], P('shape', 'query')
- key_grad: float32 [16, 1024, 512], P('shape', 'query')
- value_grad: float32 [16, 1024, 512], P('shape', 'query')
- weight_grad: float32 [512, 512], replicated
All inputs are finite; a program needn't handle non-finite values.
Results may differ from a plain program's by a relative error of at most 0.02.
Values may be sent and summed in bfloat16 or wider, within the bound.
A program may use at most 64 MiB of HBM per device.

v0:
```python
import math
import jax
import jax.numpy as jnp
from jax import lax
from jax.sharding import PartitionSpec as P

HEADS = 8
HEAD = 64


def shards(queries, keys, values, out_weight, out_grad):
    lat_rows = keys.shape[1]
    width = queries.shape[2]
    scale = 1.0 / math.sqrt(HEAD)
    shape_count = lax.axis_size("shape")
    members = lax.axis_size("query")
    query_rows = queries[0]
    grad_b = out_grad[0].astype(jnp.bfloat16)
    d_attn = jnp.einsum("tf,df->td", grad_b, out_weight, preferred_element_type=jnp.float32).astype(
        jnp.bfloat16
    )
    key_all, value_all = (
        lax.all_gather(keys[0], "query", axis=0, tiled=True),
        lax.all_gather(values[0], "query", axis=0, tiled=True),
    )
    grad_list, attn_list, key_list, value_list = ([], [], [], [])
    for head_index in range(HEADS):
        cols = slice(head_index * HEAD, (head_index + 1) * HEAD)
        q_head = query_rows[:, cols]
        key_head = key_all[:, cols]
        value_head = value_all[:, cols]
        scores = jnp.dot(q_head, key_head.T, preferred_element_type=jnp.float32) * scale
        top = jnp.max(scores, axis=1, keepdims=True)
        lse = top + jnp.log(jnp.sum(jnp.exp(scores - top), axis=1, keepdims=True))
        probs = jnp.exp(scores - lse)
        probs_b = probs.astype(jnp.bfloat16)
        attn_b = jnp.dot(probs_b, value_head, preferred_element_type=jnp.float32).astype(
            jnp.bfloat16
        )
        d_head = d_attn[:, cols]
        delta = jnp.sum(
            d_head.astype(jnp.float32) * attn_b.astype(jnp.float32), axis=1, keepdims=True
        )
        d_probs = jnp.dot(d_head, value_head.T, preferred_element_type=jnp.float32)
        d_scores = (probs * (d_probs - delta) * scale).astype(jnp.bfloat16)
        grad_list.append(jnp.dot(d_scores, key_head, preferred_element_type=jnp.float32))
        key_list.append(
            jnp.einsum("tm,td->md", d_scores, q_head, preferred_element_type=jnp.float32)
        )
        value_list.append(
            jnp.einsum("tm,td->md", probs_b, d_head, preferred_element_type=jnp.float32)
        )
        attn_list.append(attn_b)
    query_grad = jnp.concatenate(grad_list, axis=1)
    attn = jnp.concatenate(attn_list, axis=1)
    key_terms = jnp.concatenate(key_list, axis=1).reshape(members, lat_rows, width)
    value_terms = jnp.concatenate(value_list, axis=1).reshape(members, lat_rows, width)
    key_in, value_in = (
        lax.all_to_all(key_terms, "query", split_axis=0, concat_axis=0, tiled=True),
        lax.all_to_all(value_terms, "query", split_axis=0, concat_axis=0, tiled=True),
    )
    key_grad = jnp.sum(key_in, axis=0)
    value_grad = jnp.sum(value_in, axis=0)
    weight_term = jnp.einsum("td,tf->df", attn, grad_b, preferred_element_type=jnp.float32) * (
        1.0 / shape_count
    )
    weight_grad = lax.psum(weight_term, ("shape", "query"))
    return (query_grad[None], key_grad[None], value_grad[None], weight_grad)


def solution(mesh):
    return jax.shard_map(
        shards,
        mesh=mesh,
        in_specs=(
            P("shape", "query", None),
            P("shape", "query", None),
            P("shape", "query", None),
            P(),
            P("shape", "query", None),
        ),
        out_specs=(
            P("shape", "query", None),
            P("shape", "query", None),
            P("shape", "query", None),
            P(),
        ),
        check_vma=False,
    )
```

profile of v0, /device:TPU:1, one launch (start us, length us, event | category | flops | bytes accessed | tf_op | source)
XLA Modules:
  0.0 804.2 jit_solution(14749125188669435958)
XLA Ops:
  8.2 1.3 convolution_convert_fusion
  9.5 79.2 %all-gather.5.cloned.1.call-done = bf16[1,1024,512]{2,1,0:T(8,128)(2,1)} async-done(((bf16[1,32,512]{2,1,0:T(8,128)(2,1)}), bf16[1,1024,512]{2,1,0:T(8,128)(2,1)}) %all-gather.5.cloned.1.call-update) | async-done | bytes 1048592 | tf_op jit(solution)/shard_map/all_gather | solution.py:23
  88.7 1.4 fusion.117
  90.1 1.6 fusion.118
  91.6 1.5 fusion.119
  97.0 1.0 convolution_dynamic-update-slice_fusion.7
  98.0 1.0 convolution_dynamic-update-slice_fusion.6
  99.0 1.0 convolution_dynamic-update-slice_fusion.5
  100.0 1.0 convolution_dynamic-update-slice_fusion.4
  101.0 1.0 convolution_dynamic-update-slice_fusion.3
  102.0 1.0 convolution_dynamic-update-slice_fusion.2
  103.0 1.0 convolution_dynamic-update-slice_fusion.1
  104.0 1.0 convolution_dynamic-update-slice_fusion
  105.0 2.9 copy.27
  107.9 7.5 all-to-all-start.1
  116.1 140.1 %all-gather.7.cloned.1.call-done = bf16[1,1024,512]{2,1,0:T(8,128)(2,1)} async-done(((bf16[1,32,512]{2,1,0:T(8,128)(2,1)}), bf16[1,1024,512]{2,1,0:T(8,128)(2,1)}) %all-gather.7.cloned.1.call-update) | async-done | bytes 1048592 | tf_op jit(solution)/shard_map/all_gather | solution.py:24
  256.3 1.4 convolution_convert_fusion.2
  257.7 1.3 convolution_convert_fusion.3
  259.1 1.3 convolution_convert_fusion.4
  265.0 1.0 convolution_dynamic-update-slice_fusion.14
  267.5 1.0 convolution_dynamic-update-slice_fusion.12
  270.1 1.0 convolution_dynamic-update-slice_fusion.10
  272.6 1.0 convolution_dynamic-update-slice_fusion.8
  273.6 2.9 copy.26
  276.7 7.6 all-to-all-start
  284.8 2.3 convolution_multiply_fusion
  290.4 1.8 copy.28
  292.2 2.4 reduce_sum.179
  294.5 90.0 %all-to-all-done = f32[32,32,512]{2,1,0:T(8,128)} async-done(((f32[32,32,512]{2,1,0:T(8,128)}), f32[32,32,512]{2,1,0:T(8,128)}, u32[]{:S(2)}, u32[]{:S(2)}) %all-to-all-start) | async-done | bytes 2097184 | tf_op jit(solution)/shard_map/all_to_all | solution.py:59
  384.6 2.4 reduce_sum.178
  386.9 408.5 %all-reduce.2.cloned.1.call-done = f32[512,512]{1,0:T(8,128)} async-done(((f32[512,512]{1,0:T(8,128)}), f32[512,512]{1,0:T(8,128)}) %all-reduce.2.cloned.1.call-update) | async-done | bytes 1048592 | tf_op jit(solution)/shard_map/psum | solution.py:67
  795.4 2.3 copy.59
  (150 shorter events, 18.0 us)
Async XLA Ops:
  7.2 84.4 %copy-start.23 = (bf16[1,128,512]{2,1,0:T(8,128)(2,1)S(1)}, bf16[1,128,512]{2,1,0:T(8,128)(2,1)}, u32[]{:S(2)}) copy-start(bf16[1,128,512]{2,1,0:T(8,128)(2,1)} %param.5) | copy-start | bytes 393220
  7.2 81.5 %all-gather.5.cloned.1.call-start = ((), (), s32[]{:S(2)}) async-start(), calls=%async_computation.3 | async-start | bytes 1081344 | tf_op jit(solution)/shard_map/all_gather | solution.py:23
  88.7 4.4 copy-start.1
  90.0 6.9 copy-start.9
  91.6 6.4 copy-start.7
  93.1 5.9 copy-start.5
  93.5 6.5 copy-start.3
  95.0 9.0 %copy-start.11 = (f32[128,1024]{1,0:T(8,128)}, f32[128,1024]{1,0:T(8,128)S(1)}, u32[]{:S(2)}) copy-start(f32[128,1024]{1,0:T(8,128)S(1)} %get-tuple-element.21) | copy-start | bytes 1572868
  95.2 166.2 %copy-start.43 = (f32[128]{0:T(128)}, f32[128]{0:T(128)S(1)}, u32[]{:S(2)}) copy-start(f32[128]{0:T(128)S(1)} %log_add_fusion.7) | copy-start | bytes 1540
  95.5 165.6 %copy-start.44 = (f32[128]{0:T(128)}, f32[128]{0:T(128)S(1)}, u32[]{:S(2)}) copy-start(f32[128]{0:T(128)S(1)} %log_add_fusion.6) | copy-start | bytes 1540
  95.7 165.0 %copy-start.41 = (f32[128]{0:T(128)}, f32[128]{0:T(128)S(1)}, u32[]{:S(2)}) copy-start(f32[128]{0:T(128)S(1)} %log_add_fusion.5) | copy-start | bytes 1540
  97.0 164.8 %copy-start.46 = (f32[128]{0:T(128)}, f32[128]{0:T(128)S(1)}, u32[]{:S(2)}) copy-start(f32[128]{0:T(128)S(1)} %log_add_fusion) | copy-start | bytes 1540
  107.9 168.7 %all-to-all-start.1 = ((f32[32,32,512]{2,1,0:T(8,128)}), f32[32,32,512]{2,1,0:T(8,128)}, u32[]{:S(2)}, u32[]{:S(2)}) async-start(f32[32,32,512]{2,1,0:T(8,128)} %bitcast.63), calls=%async_computation.1 | async-start | bytes 4194304 | tf_op jit(solution)/shard_map/all_to_all | solution.py:60
  115.4 140.9 %all-gather.7.cloned.1.call-start = ((), (), s32[]{:S(2)}) async-start(), calls=%async_computation.4 | async-start | bytes 1081344 | tf_op jit(solution)/shard_map/all_gather | solution.py:24
  256.3 4.1 copy-start.2
  256.3 4.1 copy-start.4
  256.3 4.5 copy-start.6
  256.3 4.8 copy-start.8
  257.7 4.1 copy-start.26
  261.8 4.2 copy-start.38
  261.8 4.2 copy-start.42
  272.6 4.0 copy-start.21
  276.6 8.0 copy-start.27
  276.6 8.0 copy-start.29
  276.6 8.0 copy-start.31
  276.6 8.0 copy-start.33
  276.6 8.0 copy-start.35
  276.6 8.0 copy-start.37
  276.6 8.0 copy-start.39
  276.6 8.0 copy-start.40
  276.7 107.9 %all-to-all-start = ((f32[32,32,512]{2,1,0:T(8,128)}), f32[32,32,512]{2,1,0:T(8,128)}, u32[]{:S(2)}, u32[]{:S(2)}) async-start(f32[32,32,512]{2,1,0:T(8,128)} %bitcast.64), calls=%async_computation | async-start | bytes 4194304 | tf_op jit(solution)/shard_map/all_to_all | solution.py:59
  284.3 511.1 %all-reduce.2.cloned.1.call-start = ((), (), s32[]{:S(2)}) async-start(), calls=%async_computation.2 | async-start | bytes 2097152 | tf_op jit(solution)/shard_map/psum | solution.py:67
  (21 other events, 64.5 us)
Sparse Core Ops, SparseCore 0:
  11.2 77.4 all-gather.4
  119.4 136.8 all-gather.6
  291.2 504.1 all-reduce.1
where the time goes:
time: 805 us; the launch traced here: 804 us
  waiting for transfers between devices  719 us (89%)
  matrix products  37.1 us (5%)
  starting transfers between devices  15.4 us (2%)
  between operations  14.6 us (2%)
  local copies, waits for them, and re-layouts  11.2 us (1%)
    psum x1, waiting for transfers between devices, shards(): weight_grad = lax.psum(weight_term, ('shape', 'query'))  408 us
    all_gather x1, waiting for transfers between devices, shards(): lax.all_gather(values[0], 'query', axis=0, tiled=True)  140 us
    all_to_all x1, waiting for transfers between devices, shards(): lax.all_to_all(key_terms, 'query', split_axis=0, concat_axis=0, tiled=True)  90 us
    all_gather x1, waiting for transfers between devices, shards(): lax.all_gather(keys[0], 'query', axis=0, tiled=True)  79.2 us
  transfers between devices with their start and end apart: 5, of which 4 were waited for; matrix products, arithmetic and copies ran while one was open for 4% of the time, Pallas kernels for 0%

commit v1 on v0

--- a/solution.py
+++ b/solution.py
@@ -64,7 +64,8 @@
     weight_term = jnp.einsum("td,tf->df", attn, grad_b, preferred_element_type=jnp.float32) * (
         1.0 / shape_count
     )
-    weight_grad = lax.psum(weight_term, ("shape", "query"))
+    partial = lax.psum(weight_term, "shape")
+    weight_grad = lax.psum(partial, "query")
     return (query_grad[None], key_grad[None], value_grad[None], weight_grad)
 
 

time: 805 us -> 863 us (1.072)
  waiting for transfers between devices: 719 us -> 775 us
    psum x1 -> x2, waiting for transfers between devices: 408 us -> 555 us  [the longest x1 352 us: shards(): weight_grad = lax.psum(partial, 'query')]
    all_to_all x1, waiting for transfers between devices: 90 us -> 0.01 us  [shards(): lax.all_to_all(key_terms, 'query', split_axis=0, concat_axis=0, tiled=True)]
  transfers between devices with their start and end apart: 5 -> 6, of which waited for: 4 -> 4; matrix products, arithmetic and copies ran while one was open for 4% -> 4% of each run, Pallas kernels for 0% -> 0%
where the time goes in v1:
time: 863 us
  waiting for transfers between devices  775 us (90%)
  matrix products  40.3 us (5%)
  starting transfers between devices  15.3 us (2%)
  between operations  14.5 us (2%)
  local copies, waits for them, and re-layouts  10.5 us (1%)
    psum x1, waiting for transfers between devices, shards(): weight_grad = lax.psum(partial, 'query')  352 us
    psum x1, waiting for transfers between devices, shards(): partial = lax.psum(weight_term, 'shape')  203 us
    all_gather x1, waiting for transfers between devices, shards(): lax.all_gather(values[0], 'query', axis=0, tiled=True)  140 us
    all_gather x1, waiting for transfers between devices, shards(): lax.all_gather(keys[0], 'query', axis=0, tiled=True)  79.2 us
  transfers between devices with their start and end apart: 6, of which 4 were waited for; matrix products, arithmetic and copies ran while one was open for 4% of the time, Pallas kernels for 0%

profile of v1, /device:TPU:1, one launch (start us, length us, event | category | flops | bytes accessed | tf_op | source)
XLA Modules:
  0.0 862.7 jit_solution(14418367302656456988)
XLA Ops:
  8.2 1.3 convolution_convert_fusion
  9.5 79.2 %all-gather.5.cloned.1.call-done = bf16[1,1024,512]{2,1,0:T(8,128)(2,1)} async-done(((bf16[1,32,512]{2,1,0:T(8,128)(2,1)}), bf16[1,1024,512]{2,1,0:T(8,128)(2,1)}) %all-gather.5.cloned.1.call-update) | async-done | bytes 1048592 | tf_op jit(solution)/shard_map/all_gather | solution.py:23
  88.7 1.4 fusion.117
  90.0 1.6 fusion.118
  91.6 1.5 fusion.119
  98.0 1.0 convolution_dynamic-update-slice_fusion.6
  99.0 1.0 convolution_dynamic-update-slice_fusion.5
  100.0 1.0 convolution_dynamic-update-slice_fusion.4
  101.0 1.0 convolution_dynamic-update-slice_fusion.3
  102.0 1.0 convolution_dynamic-update-slice_fusion.2
  103.0 1.0 convolution_dynamic-update-slice_fusion.1
  104.0 1.0 convolution_dynamic-update-slice_fusion
  105.0 2.9 copy.27
  107.9 7.5 all-to-all-start.1
  116.1 139.8 %all-gather.7.cloned.1.call-done = bf16[1,1024,512]{2,1,0:T(8,128)(2,1)} async-done(((bf16[1,32,512]{2,1,0:T(8,128)(2,1)}), bf16[1,1024,512]{2,1,0:T(8,128)(2,1)}) %all-gather.7.cloned.1.call-update) | async-done | bytes 1048592 | tf_op jit(solution)/shard_map/all_gather | solution.py:24
  255.9 1.4 convolution_convert_fusion.2
  257.3 1.3 convolution_convert_fusion.3
  258.7 1.3 convolution_convert_fusion.4
  263.9 1.0 convolution_dynamic-update-slice_fusion.14
  266.5 1.0 convolution_dynamic-update-slice_fusion.12
  269.1 1.0 convolution_dynamic-update-slice_fusion.10
  271.6 1.0 convolution_dynamic-update-slice_fusion.8
  272.6 2.9 copy.26
  275.6 7.6 all-to-all-start
  283.6 1.3 convolution_multiply_fusion
  285.8 1.0 convolution_dynamic-update-slice_fusion.22
  287.7 203.1 %all-reduce.3.cloned.1.call-done = f32[512,512]{1,0:T(8,128)} async-done(((f32[512,512]{1,0:T(8,128)}), f32[512,512]{1,0:T(8,128)}) %all-reduce.3.cloned.1.call-update) | async-done | bytes 1048592 | tf_op jit(solution)/shard_map/psum | solution.py:67
  495.5 1.8 copy.28
  497.3 2.4 reduce_sum.179
  499.6 2.4 reduce_sum.178
  502.0 352.0 %all-reduce.5.cloned.1.call-done = f32[512,512]{1,0:T(8,128)} async-done(((f32[512,512]{1,0:T(8,128)}), f32[512,512]{1,0:T(8,128)}) %all-reduce.5.cloned.1.call-update) | async-done | bytes 1048592 | tf_op jit(solution)/shard_map/psum | solution.py:68
  854.0 2.3 copy.60
  (147 shorter events, 21.5 us)
Async XLA Ops:
  7.2 84.4 %copy-start.25 = (bf16[1,128,512]{2,1,0:T(8,128)(2,1)S(1)}, bf16[1,128,512]{2,1,0:T(8,128)(2,1)}, u32[]{:S(2)}) copy-start(bf16[1,128,512]{2,1,0:T(8,128)(2,1)} %param.5) | copy-start | bytes 393220
  7.2 81.5 %all-gather.5.cloned.1.call-start = ((), (), s32[]{:S(2)}) async-start(), calls=%async_computation.4 | async-start | bytes 1081344 | tf_op jit(solution)/shard_map/all_gather | solution.py:23
  88.7 4.4 copy-start.1
  90.0 6.9 copy-start.9
  91.6 6.3 copy-start.7
  93.1 5.9 copy-start.5
  93.5 6.5 copy-start.3
  95.0 9.0 %copy-start.11 = (f32[128,1024]{1,0:T(8,128)}, f32[128,1024]{1,0:T(8,128)S(1)}, u32[]{:S(2)}) copy-start(f32[128,1024]{1,0:T(8,128)S(1)} %get-tuple-element.21) | copy-start | bytes 1572868
  97.0 164.4 %copy-start.43 = (f32[128]{0:T(128)}, f32[128]{0:T(128)S(1)}, u32[]{:S(2)}) copy-start(f32[128]{0:T(128)S(1)} %log_add_fusion) | copy-start | bytes 1540
  107.9 167.7 %all-to-all-start.1 = ((f32[32,32,512]{2,1,0:T(8,128)}), f32[32,32,512]{2,1,0:T(8,128)}, u32[]{:S(2)}, u32[]{:S(2)}) async-start(f32[32,32,512]{2,1,0:T(8,128)} %bitcast.63), calls=%async_computation.1 | async-start | bytes 4194304 | tf_op jit(solution)/shard_map/all_to_all | solution.py:60
  115.4 140.5 %all-gather.7.cloned.1.call-start = ((), (), s32[]{:S(2)}) async-start(), calls=%async_computation.5 | async-start | bytes 1081344 | tf_op jit(solution)/shard_map/all_gather | solution.py:24
  255.9 4.1 copy-start.2
  255.9 4.1 copy-start.4
  255.9 4.5 copy-start.6
  255.9 4.8 copy-start.8
  257.3 4.1 copy-start.28
  271.6 4.0 copy-start.23
  275.5 7.8 copy-start.29
  275.5 7.8 copy-start.31
  275.6 7.8 copy-start.33
  275.6 7.8 copy-start.35
  275.6 7.8 copy-start.37
  275.6 7.8 copy-start.39
  275.6 7.8 copy-start.41
  275.6 7.8 copy-start.42
  275.6 8.0 copy-start.27
  275.6 224.0 %all-to-all-start = ((f32[32,32,512]{2,1,0:T(8,128)}), f32[32,32,512]{2,1,0:T(8,128)}, u32[]{:S(2)}, u32[]{:S(2)}) async-start(f32[32,32,512]{2,1,0:T(8,128)} %bitcast.64), calls=%async_computation | async-start | bytes 4194304 | tf_op jit(solution)/shard_map/all_to_all | solution.py:59
  283.3 207.5 %all-reduce.3.cloned.1.call-start = ((), (), s32[]{:S(2)}) async-start(), calls=%async_computation.2 | async-start | bytes 2097152 | tf_op jit(solution)/shard_map/psum | solution.py:67
  284.9 206.9 %copy-start.16 = (bf16[128,1024]{1,0:T(8,128)(2,1)S(1)}, bf16[128,1024]{1,0:T(8,128)(2,1)}, u32[]{:S(2)}) copy-start(bf16[128,1024]{1,0:T(8,128)(2,1)} %copy-done.15) | copy-start | bytes 786436
  284.9 207.8 %copy-start.20 = (bf16[128,1024]{1,0:T(8,128)(2,1)S(1)}, bf16[128,1024]{1,0:T(8,128)(2,1)}, u32[]{:S(2)}) copy-start(bf16[128,1024]{1,0:T(8,128)(2,1)} %copy-done.19) | copy-start | bytes 786436
  284.9 569.1 %all-reduce.5.cloned.1.call-start = ((), (), s32[]{:S(2)}) async-start(), calls=%async_computation.3 | async-start | bytes 2097152 | tf_op jit(solution)/shard_map/psum | solution.py:68
  285.8 208.7 %copy-start.24 = (bf16[128,1024]{1,0:T(8,128)(2,1)S(1)}, bf16[128,1024]{1,0:T(8,128)(2,1)}, u32[]{:S(2)}) copy-start(bf16[128,1024]{1,0:T(8,128)(2,1)} %copy-done.23) | copy-start | bytes 786436
  (19 other events, 51.4 us)
Sparse Core Ops, SparseCore 0:
  11.2 77.4 all-gather.4
  119.4 136.5 all-gather.6
  287.6 203.1 all-reduce.2
  493.8 360.0 all-reduce.4
